TPU v7x, 512 devices: a whole 4x4x16 slice. The times are simulated.
512 devices in a mesh: dp: 64 (over z, x), sub: 8 (over y, core).
Axes of the slice: x: 4, y: 4, z: 16, core: 2. Of those that a mesh axis runs over, the one named last changes fastest.
Arguments:
- points: bfloat16 [262144, 256], P(('dp', 'sub'))
- candidates: int32 [4, 768], replicated, may hold values from 0 to 262143, as said below
- owner_slot: int32 [3072], replicated, may hold values from 0 to 3071, each once
Outputs:
- centroids: float32 [3072, 256], P(('dp', 'sub'))
- masses: float32 [3072], P(('dp', 'sub'))
- min_dist: float32 [262144], P(('dp', 'sub'))
Inputs may be any that keep to these rules, and one draw needn't show every extreme that they name: In each round the candidates are distinct rows; no device's block of 512 rows holds more than 8 candidates of one round, and in each round some device's block holds exactly 8.
All inputs are finite; a program needn't handle non-finite values.
Results may differ from a plain program's by a relative error of at most 0.00055.
Values may be sent and summed in bfloat16 or wider, within the bound.
A program may use at most 64 MiB of HBM per device.

v0:
```python
import jax
import jax.numpy as jnp
from jax import lax
from jax.sharding import PartitionSpec as P


def pick_rows(round_rows, points, my_device):
    row_count = points.shape[0]
    flat_rows = round_rows.reshape(-1)
    owner_dev = flat_rows // row_count
    local_row = flat_rows % row_count
    mine = owner_dev == my_device
    picked = jnp.where(
        mine[:, None], points[local_row].astype(jnp.float32), jnp.zeros((), jnp.float32)
    )
    return lax.psum(picked, ("dp", "sub")).astype(jnp.bfloat16)


def on_device(points, candidates, owner_slot):
    row_count = points.shape[0]
    width_dim = points.shape[1]
    round_count = candidates.shape[0]
    my_device = lax.axis_index(("dp", "sub"))
    block_rows = min(512, row_count)
    point_norm = jnp.sum(points.astype(jnp.float32) ** 2, axis=1)
    chosen_list = [
        pick_rows(candidates[which_round : which_round + 1], points, my_device)
        for which_round in range(round_count)
    ]
    nearest_parts = [jnp.full((block_rows,), 3e38, jnp.float32)]
    sums_parts = []
    mass_parts = []
    for which_round in range(round_count):
        chosen = chosen_list[which_round]
        cand_norm = jnp.sum(chosen.astype(jnp.float32) ** 2, axis=1)
        dots = lax.dot_general(
            points, chosen, (((1,), (1,)), ((), ())), preferred_element_type=jnp.float32
        )
        dist = point_norm[:, None] + cand_norm[None, :] - 2.0 * dots
        nearest_parts[0] = jnp.minimum(nearest_parts[0], jnp.min(dist, axis=1))
        kernel = jnp.exp(-dist / 0.25).astype(jnp.bfloat16)
        sums_round = lax.dot_general(
            kernel, points, (((0,), (0,)), ((), ())), preferred_element_type=jnp.float32
        )
        mass_round = jnp.sum(kernel.astype(jnp.float32), axis=0)
        sums_parts.append(sums_round)
        mass_parts.append(mass_round)
    partial_sums = jnp.concatenate(sums_parts, axis=0)
    partial_mass = jnp.concatenate(mass_parts, axis=0)
    total_rows = partial_sums.shape[0]
    placed_sums = jnp.zeros((total_rows, width_dim), jnp.float32).at[owner_slot].set(partial_sums)
    placed_mass = jnp.zeros((total_rows,), jnp.float32).at[owner_slot].set(partial_mass)
    summed, masses = (
        lax.psum_scatter(placed_sums, ("dp", "sub"), scatter_dimension=0, tiled=True),
        lax.psum_scatter(placed_mass, ("dp", "sub"), scatter_dimension=0, tiled=True),
    )
    centroids = summed / masses[:, None]
    min_dist = nearest_parts[0]
    return (centroids, masses, min_dist)


def solution(mesh):
    placed = (P(("dp", "sub"), None), P(), P())
    return jax.shard_map(
        on_device,
        mesh=mesh,
        in_specs=placed,
        out_specs=(P(("dp", "sub"), None), P(("dp", "sub")), P(("dp", "sub"))),
        check_vma=False,
    )
```

profile of v0, /device:TPU:2, one launch (start us, length us, event | category | flops | bytes accessed | tf_op | source)
XLA Modules:
  0.0 728.4 jit_solution(3182562303138796579)
XLA Ops:
  7.2 0.0 copy-start
  7.2 0.0 all-reduce.6.cloned.1.call-start
  7.2 0.9 slice_reduce_fusion.3
  8.1 0.9 fusion.31
  9.1 1.1 multiply_reduce_fusion.4
  10.2 0.7 compare_select_fusion
  10.9 0.0 copy-done
  10.9 2.7 gather_fusion.3
  13.6 2.7 gather_fusion.1
  16.3 0.2 convert_select_fusion.2
  16.5 0.2 convert_select_fusion
  16.6 2.7 gather_fusion.2
  19.3 0.2 convert_select_fusion.1
  19.5 3.3 gather_fusion
  22.8 1.2 convert_select_fusion.3
  23.9 188.3 %all-reduce.7 = (bf16[768,256]{1,0:T(8,128)(2,1)}, bf16[768,256]{1,0:T(8,128)(2,1)}, bf16[768,256]{1,0:T(8,128)(2,1)}, bf16[768,256]{1,0:T(8,128)(2,1)}) all-reduce(f32[768,256]{1,0:T(8,128)S(1)} %convert_select_fusion, f32[768,256]{1,0:T(8,128)S(1)} %convert_select_fusion.1, ...), channel_id=1, replica_groups=mesh['dp'=64,'sub'=8] {'dp','sub'}, use_global_device_ids=true, to_apply=%region_7.8 | all-reduce | flops 786432 | bytes 4718592 | tf_op jit(solution)/shard_map/psum | solution.py:16
  212.2 0.0 copy-start.4
  212.2 1.2 multiply_reduce_fusion
  213.4 1.2 multiply_reduce_fusion.1
  214.6 1.2 multiply_reduce_fusion.2
  215.8 1.2 multiply_reduce_fusion.3
  217.0 0.0 copy-done.4
  217.0 0.7 fusion.43
  217.7 0.0 copy-start.3
  217.7 0.4 fusion.13
  218.1 0.6 copy-done.3
  218.7 0.7 fusion.44
  219.4 0.0 copy-start.2
  219.4 0.4 fusion.14
  219.7 0.6 copy-done.2
  220.4 0.7 fusion.45
  221.0 0.0 copy-start.1
  221.0 0.4 fusion.15
  221.4 0.6 copy-done.1
  222.0 0.7 fusion.46
  222.7 0.4 fusion.16
  223.1 17.2 %scatter_custom_fusion = f32[3072,256]{1,0:T(8,128)} fusion(s32[3072]{0:T(1024)S(1)} %compare_select_fusion, f32[768,256]{1,0:T(8,128)S(1)} %fusion.16, f32[]{:T(128)} %constant.110, f32[768,256]{1,0:T(8,128)S(1)} %fusion.15, f32[768,256]{1,0:T(8,128)S(1)} %fusion.14, f32[768,256]{1,0:T(8,128)S(1)} %fusion.13, f32[]{:T(128)} %constant.80.clone.1), kind=kCustom, calls=%fused_computation.6 | custom fusion | flops 2359296 | bytes 6291464 | tf_op jit(solution)/shard_map/scatter | solution.py:51
  240.3 0.0 all-reduce.6.cloned.1.call-update
  240.3 11.8 %scatter_custom_fusion.1 = f32[3072]{0:T(1024)S(1)} fusion(s32[3072]{0:T(1024)S(1)} %compare_select_fusion, f32[3072]{0:T(1024)S(1)} %pad_maximum_fusion, f32[]{:T(128)} %constant.80.clone.1), kind=kCustom, calls=%fused_computation.63 | custom fusion | bytes 12292 | tf_op jit(solution)/shard_map/scatter | solution.py:52
  252.1 100.5 %all-reduce.1 = f32[3072]{0:T(1024)S(1)} all-reduce(f32[3072]{0:T(1024)S(1)} %scatter_custom_fusion.1), channel_id=3, replica_groups=mesh['dp'=64,'sub'=8] {'dp','sub'}, use_global_device_ids=true, to_apply=%region_16.17.clone | all-reduce | flops 3072 | bytes 24576
  352.7 0.1 dynamic-slice.1
  352.8 0.0 copy-start.5
  352.8 0.6 minimum_minimum_fusion
  353.3 366.8 %all-reduce.6.cloned.1.call-done = f32[3072,256]{1,0:T(8,128)} async-done(((f32[3072,256]{1,0:T(8,128)}), f32[3072,256]{1,0:T(8,128)}) %all-reduce.6.cloned.1.call-update) | async-done | bytes 3145744
  720.1 1.4 dynamic-slice_divide_fusion
  721.5 0.0 copy-done.5
  (5 shorter events, 0.0 us)
Async XLA Ops:
  7.2 3.7 copy-start
  7.2 712.9 %all-reduce.6.cloned.1.call-start = ((), (), s32[]{:S(2)}) async-start(), calls=%async_computation | async-start | bytes 6291456
  212.2 4.8 copy-start.4
  217.7 1.0 copy-start.3
  219.4 1.0 copy-start.2
  221.0 1.0 copy-start.1
  352.8 368.8 %copy-start.5 = (f32[6]{0:T(128)}, f32[6]{0:T(128)S(1)}, u32[]{:S(2)}) copy-start(f32[6]{0:T(128)S(1)} %dynamic-slice.1) | copy-start | bytes 76
Sparse Core Ops, SparseCore 0:
  240.4 479.6 all-reduce.5
where the time goes:
time: 729 us; the launch traced here: 728 us
  waiting for transfers between devices  367 us (50%)
  blocking collectives  289 us (40%)
  other arithmetic  28.4 us (4%)
  local copies, waits for them, and re-layouts  25.9 us (4%)
  between operations  14.3 us (2%)
    unnamed x2, waiting for transfers between devices  367 us
    psum x1, blocking collectives, pick_rows(): return lax.psum(picked, ('dp', 'sub')).astype(jnp.bfloat16)  188 us
    unnamed x1, blocking collectives  101 us
    scatter x1, other arithmetic, on_device(): jnp.zeros((total_rows, width_dim), jnp.float32).at[owner_slot]  17.2 us
  transfers between devices with their start and end apart: 1, of which 1 were waited for; matrix products, arithmetic and copies ran while one was open for 2% of the time, Pallas kernels for 0%

commit v1 on v0

--- a/solution.py
+++ b/solution.py
@@ -13,7 +13,7 @@
     picked = jnp.where(
         mine[:, None], points[local_row].astype(jnp.float32), jnp.zeros((), jnp.float32)
     )
-    return lax.psum(picked, ("dp", "sub")).astype(jnp.bfloat16)
+    return lax.psum(lax.psum(picked, "sub"), "dp").astype(jnp.bfloat16)
 
 
 def on_device(points, candidates, owner_slot):

time: 729 us -> 940 us (1.29)
  blocking collectives: 289 us -> 414 us
  waiting for transfers between devices: 367 us -> 457 us
    psum x1, blocking collectives: 188 us -> 311 us  [pick_rows(): return lax.psum(lax.psum(picked, 'sub'), 'dp').astype(jnp.bfloat16)]
    psum x0 -> x1, waiting for transfers between devices: none -> 88.7 us  [pick_rows(): return lax.psum(lax.psum(picked, 'sub'), 'dp').astype(jnp.bfloat16)]
    unnamed x2 -> x3, waiting for transfers between devices: 367 us -> 368 us
  transfers between devices with their start and end apart: 1 -> 2, of which waited for: 1 -> 2; matrix products, arithmetic and copies ran while one was open for 2% -> 1% of each run, Pallas kernels for 0% -> 0%
where the time goes in v1:
time: 940 us; the launch traced here: 939 us
  waiting for transfers between devices  457 us (49%)
  blocking collectives  414 us (44%)
  other arithmetic  25.3 us (3%)
  local copies, waits for them, and re-layouts  24.4 us (3%)
  between operations  14.2 us (2%)
    unnamed x3, waiting for transfers between devices  368 us
    psum x1, blocking collectives, pick_rows(): return lax.psum(lax.psum(picked, 'sub'), 'dp').astype(jnp.bfloat16)  311 us
    unnamed x1, blocking collectives  103 us
    psum x1, waiting for transfers between devices, pick_rows(): return lax.psum(lax.psum(picked, 'sub'), 'dp').astype(jnp.bfloat16)  88.7 us
  transfers between devices with their start and end apart: 2, of which 2 were waited for; matrix products, arithmetic and copies ran while one was open for 1% of the time, Pallas kernels for 0%

profile of v1, /device:TPU:2, one launch (start us, length us, event | category | flops | bytes accessed | tf_op | source)
XLA Modules:
  0.0 939.3 jit_solution(9356428414461727601)
XLA Ops:
  7.2 0.0 all-reduce.10.cloned.1.call-start
  7.2 0.9 slice_reduce_fusion.3
  8.1 0.9 fusion.31
  9.1 0.0 copy-start
  9.1 3.1 gather_fusion.3
  12.2 0.0 copy-done
  12.3 2.7 gather_fusion.1
  14.9 2.7 gather_fusion.2
  17.6 2.7 gather_fusion
  20.3 1.1 convert_select_fusion.2
  21.4 1.0 convert_select_fusion
  22.4 1.0 convert_select_fusion.1
  23.5 1.1 convert_select_fusion.3
  24.6 0.0 copy-start.1
  24.6 0.0 all-reduce.10.cloned.1.call-update
  24.6 0.0 all-reduce.8.cloned.1.call-start
  24.6 0.1 multiply_reduce_fusion.4
  24.8 0.5 copy-done.1
  25.3 88.7 %all-reduce.10.cloned.1.call-done = (f32[768,256]{1,0:T(8,128)}, f32[768,256]{1,0:T(8,128)}, f32[768,256]{1,0:T(8,128)}, f32[768,256]{1,0:T(8,128)}) async-done(((f32[768,256]{1,0:T(8,128)}, f32[768,256]{1,0:T(8,128)}, f32[768,256]{1,0:T(8,128)}, f32[768,256]{1,0:T(8,128)}), (f32[768,256]{1,0:T(8,128)}, f32[768,256]{1,0:T(8,128)}, f32[768,256]{1,0:T(8,128)}, ...) | async-done | bytes 3145744 | tf_op jit(solution)/shard_map/psum | solution.py:16
  113.9 310.9 %all-reduce.11 = (bf16[768,256]{1,0:T(8,128)(2,1)S(1)}, bf16[768,256]{1,0:T(8,128)(2,1)S(1)}, bf16[768,256]{1,0:T(8,128)(2,1)S(1)}, bf16[768,256]{1,0:T(8,128)(2,1)S(1)}) all-reduce(f32[768,256]{1,0:T(8,128)} %get-tuple-element.23, f32[768,256]{1,0:T(8,128)} %get-tuple-element.24, ...), channel_id=1, replica_groups=mesh['dp'=64,'sub'=8] {'dp'}, use_global_device_ids=true, to_apply=%region_11.12 | all-reduce | flops 786432 | bytes 4718592 | tf_op jit(solution)/shard_map/psum | solution.py:16
  424.9 0.2 multiply_reduce_fusion
  425.0 0.2 multiply_reduce_fusion.1
  425.2 0.2 multiply_reduce_fusion.2
  425.4 0.2 multiply_reduce_fusion.3
  425.6 0.7 fusion.43
  426.3 0.4 fusion.13
  426.7 0.7 fusion.44
  427.4 0.4 fusion.14
  427.7 0.7 fusion.45
  428.4 0.4 fusion.15
  428.8 0.7 fusion.46
  429.5 0.4 fusion.16
  429.9 17.2 %scatter_custom_fusion = f32[3072,256]{1,0:T(8,128)} fusion(s32[3072]{0:T(1024)S(1)} %compare_select_fusion, f32[768,256]{1,0:T(8,128)S(1)} %fusion.16, f32[]{:T(128)} %constant.110, f32[768,256]{1,0:T(8,128)S(1)} %fusion.15, f32[768,256]{1,0:T(8,128)S(1)} %fusion.14, f32[768,256]{1,0:T(8,128)S(1)} %fusion.13, f32[]{:T(128)} %constant.80.clone.1), kind=kCustom, calls=%fused_computation.6 | custom fusion | flops 2359296 | bytes 6291464 | tf_op jit(solution)/shard_map/scatter | solution.py:51
  447.1 0.0 all-reduce.8.cloned.1.call-update
  447.1 11.8 %scatter_custom_fusion.1 = f32[3072]{0:T(1024)S(1)} fusion(s32[3072]{0:T(1024)S(1)} %compare_select_fusion, f32[3072]{0:T(1024)S(1)} %pad_maximum_fusion, f32[]{:T(128)} %constant.80.clone.1), kind=kCustom, calls=%fused_computation.63 | custom fusion | bytes 12292 | tf_op jit(solution)/shard_map/scatter | solution.py:52
  458.9 103.5 %all-reduce.1 = f32[3072]{0:T(1024)S(1)} all-reduce(f32[3072]{0:T(1024)S(1)} %scatter_custom_fusion.1), channel_id=3, replica_groups=mesh['dp'=64,'sub'=8] {'dp','sub'}, use_global_device_ids=true, to_apply=%region_20.21.clone | all-reduce | flops 3072 | bytes 24576
  562.4 0.1 dynamic-slice.1
  562.5 0.0 copy-start.2
  562.5 0.6 minimum_minimum_fusion
  563.1 368.0 %all-reduce.8.cloned.1.call-done = f32[3072,256]{1,0:T(8,128)} async-done(((f32[3072,256]{1,0:T(8,128)}), f32[3072,256]{1,0:T(8,128)}) %all-reduce.8.cloned.1.call-update) | async-done | bytes 3145744
  931.1 1.4 dynamic-slice_divide_fusion
  932.5 0.0 copy-done.2
  (6 shorter events, 0.1 us)
Async XLA Ops:
  7.2 106.8 %all-reduce.10.cloned.1.call-start = ((), (), s32[]{:S(2)}) async-start(), calls=%async_computation.1 | async-start | bytes 6291456 | tf_op jit(solution)/shard_map/psum | solution.py:16
  9.1 3.2 copy-start
  24.6 0.7 copy-start.1
  24.6 906.5 %all-reduce.8.cloned.1.call-start = ((), (), s32[]{:S(2)}) async-start(), calls=%async_computation | async-start | bytes 6291456
  562.5 370.0 %copy-start.2 = (f32[6]{0:T(128)}, f32[6]{0:T(128)S(1)}, u32[]{:S(2)}) copy-start(f32[6]{0:T(128)S(1)} %dynamic-slice.1) | copy-start | bytes 76
Sparse Core Ops, SparseCore 0:
  24.7 89.1 all-reduce.9
  447.2 483.8 all-reduce.7
